TPU v7x, 128 devices: a whole 4x4x4 slice. The times are simulated.
128 devices in a mesh: seg: 8 (over x_hi, z), seq: 16 (over x_lo, y, core).
Axes of the slice: x: 4 (x_hi: 2, x_lo: 2; x = x_hi * 2 + x_lo), y: 4, z: 4, core: 2. Of those that a mesh axis runs over, the one named last changes fastest.
Arguments:
- keyframe_latents: bfloat16 [8, 2048, 1536], P('seg', 'seq'), may hold values from -24 to 24
- keyframe_steps: int32 [8], P('seg'), may hold values from 0 to 63
- infill_latents: bfloat16 [8, 2, 2048, 1536], P('seg', None, 'seq'), may hold values from -24 to 24
- infill_steps: int32 [8, 2], P('seg'), may hold values from 0 to 63
- bounds: int32 [8, 2], P('seg'), may hold values from 0 to 7, as said below
- shift_table: float32 [64, 1536], replicated, may hold values from -4 to 4
- scale_table: float32 [64, 1536], replicated, may hold values from -0.5 to 1.5
- gate_table: float32 [64, 1536], replicated, may hold values from 0.5 to 2.5
- query_weight: bfloat16 [1536, 2048], P(None, 'seq'), may hold values from -0.15625 to 0.15625
- key_weight: bfloat16 [1536, 2048], P(None, 'seq'), may hold values from -0.15625 to 0.15625
- value_weight: bfloat16 [1536, 2048], P(None, 'seq'), may hold values from -0.15625 to 0.15625
- out_weight: bfloat16 [2048, 1536], P('seq'), may hold values from -0.125 to 0.125
- query_gain: float32 [128], replicated, may hold values from 0.5 to 2
- key_gain: float32 [128], replicated, may hold values from 0.5 to 2
Outputs:
- keyframe_out: bfloat16 [8, 2048, 1536], P('seg', 'seq')
- infill_out: bfloat16 [8, 2, 2048, 1536], P('seg', None, 'seq')
Inputs may be any that keep to these rules, and one draw needn't show every extreme that they name: `bounds`: the two keyframes of a segment differ.
All inputs are finite; a program needn't handle non-finite values.
Results may differ from a plain program's by a relative error of at most 0.0052.
Values may be sent and summed in bfloat16 or wider, within the bound.
A program may use at most 192 MiB of HBM per device.

v0:
```python
import math
import jax
import jax.numpy as jnp
from jax import lax
from jax.sharding import PartitionSpec as P

HEAD = 128
EPSILON = 1e-06


def lookup(steps, table):
    entries = table.shape[0]
    onehot = (steps[:, None] == jnp.arange(entries, dtype=jnp.int32)[None, :]).astype(jnp.float32)
    return jnp.dot(onehot, table, precision=lax.Precision.HIGHEST)


def modulate(latents, steps, shift_table, scale_table):
    shifts = lookup(steps, shift_table)
    scales = lookup(steps, scale_table)
    values = latents.astype(jnp.float32)
    center = values - jnp.mean(values, axis=-1, keepdims=True)
    normed = center * lax.rsqrt(jnp.mean(center * center, axis=-1, keepdims=True) + EPSILON)
    return (normed * (1.0 + scales[:, None, :]) + shifts[:, None, :]).astype(jnp.bfloat16)


def head_norm(projected, gain):
    flat_rows = projected.shape[0]
    shaped = projected.reshape(flat_rows, -1, gain.shape[0])
    normed = shaped * lax.rsqrt(jnp.mean(shaped * shaped, axis=-1, keepdims=True) + EPSILON) * gain
    return normed.reshape(flat_rows, -1).astype(jnp.bfloat16)


def project(modded, query_weight, key_weight, value_weight, query_gain, key_gain):
    frames, tokens, features = modded.shape
    flat = modded.reshape(frames * tokens, features)
    query_rows = head_norm(
        jnp.dot(flat, query_weight, preferred_element_type=jnp.float32), query_gain
    )
    key_rows = head_norm(jnp.dot(flat, key_weight, preferred_element_type=jnp.float32), key_gain)
    value_rows = jnp.dot(flat, value_weight, preferred_element_type=jnp.float32).astype(
        jnp.bfloat16
    )
    stacked = jnp.stack([query_rows, key_rows, value_rows], axis=1)
    return stacked.reshape(frames, tokens, 3, -1)


def attend(query_rows, key_rows, value_rows):
    length, columns = query_rows.shape
    head_count = columns // HEAD
    block_rows = math.gcd(512, length)
    query_blocks = query_rows.reshape(length // block_rows, block_rows, head_count, HEAD)
    key_heads = key_rows.reshape(-1, head_count, HEAD)
    value_heads = value_rows.reshape(-1, head_count, HEAD)

    def one_block(queries):
        scores = jnp.einsum(
            "qhd,khd->hqk", queries, key_heads, preferred_element_type=jnp.float32
        ) * (1.0 / math.sqrt(HEAD))
        powers = jnp.exp(scores)
        weights = (powers / jnp.sum(powers, axis=-1, keepdims=True)).astype(jnp.bfloat16)
        return jnp.einsum(
            "hqk,khd->qhd", weights, value_heads, preferred_element_type=jnp.float32
        ).astype(jnp.bfloat16)

    return lax.map(one_block, query_blocks).reshape(length, columns)


def local(
    keyframe_latents,
    keyframe_steps,
    infill_latents,
    infill_steps,
    bounds,
    shift_table,
    scale_table,
    gate_table,
    query_weight,
    key_weight,
    value_weight,
    out_weight,
    query_gain,
    key_gain,
):
    out_full = lax.all_gather(out_weight, "seq", axis=0, tiled=True)

    def to_heads(modded):
        return project(
            lax.all_gather(modded, "seq", axis=1, tiled=True),
            query_weight,
            key_weight,
            value_weight,
            query_gain,
            key_gain,
        )

    def finish(latents, steps, heads_out):
        token_side = lax.all_to_all(heads_out, "seq", split_axis=1, concat_axis=2, tiled=True)
        frames, tokens, columns = token_side.shape
        branch = jnp.dot(
            token_side.reshape(frames * tokens, columns),
            out_full,
            preferred_element_type=jnp.float32,
        ).reshape(latents.shape)
        gates = lookup(steps, gate_table)
        return (latents.astype(jnp.float32) + gates[:, None, :] * branch).astype(jnp.bfloat16)

    key_heads = to_heads(modulate(keyframe_latents, keyframe_steps, shift_table, scale_table))
    key_att = lax.map(
        lambda frame_data: attend(frame_data[:, 0], frame_data[:, 1], frame_data[:, 2]), key_heads
    )
    keyframe_out = finish(keyframe_latents, keyframe_steps, key_att)
    cond_all = lax.all_gather(key_heads[:, :, 1:], "seg", axis=0, tiled=True)
    segment_count = bounds.shape[0]
    length = cond_all.shape[1]
    picked = jnp.take(cond_all, bounds.reshape(-1), axis=0)
    picked = picked.reshape(segment_count, 2 * length, 2, cond_all.shape[3])
    frames = infill_latents.shape[1]
    flat_latents = infill_latents.reshape(
        segment_count * frames, infill_latents.shape[2], infill_latents.shape[3]
    )
    flat_steps = infill_steps.reshape(-1)
    infill_heads = to_heads(modulate(flat_latents, flat_steps, shift_table, scale_table))
    bounding = jnp.repeat(picked, frames, axis=0)

    def infill_frame(bundle):
        own_frame, cond_frame = bundle
        key_rows = jnp.concatenate([own_frame[:, 1], cond_frame[:, 0]], axis=0)
        value_rows = jnp.concatenate([own_frame[:, 2], cond_frame[:, 1]], axis=0)
        return attend(own_frame[:, 0], key_rows, value_rows)

    infill_att = lax.map(infill_frame, (infill_heads, bounding))
    infill_out = finish(flat_latents, flat_steps, infill_att).reshape(infill_latents.shape)
    return (keyframe_out, infill_out)


def solution(mesh):
    return jax.shard_map(
        local,
        mesh=mesh,
        in_specs=(
            P("seg", "seq", None),
            P("seg"),
            P("seg", None, "seq", None),
            P("seg", None),
            P("seg", None),
            P(),
            P(),
            P(),
            P(None, "seq"),
            P(None, "seq"),
            P(None, "seq"),
            P("seq", None),
            P(),
            P(),
        ),
        out_specs=(P("seg", "seq", None), P("seg", None, "seq", None)),
        check_vma=False,
    )
```

profile of v0, /device:TPU:1, one launch (start us, length us, event | category | flops | bytes accessed | tf_op | source)
XLA Modules:
  0.0 350.8 jit_solution(5878969197463367039)
XLA Ops:
  17.6 43.5 %all-gather.5.cloned.1.call-done = bf16[1,2048,1536]{2,1,0:T(8,128)(2,1)} async-done(((bf16[1,128,1536]{2,1,0:T(8,128)(2,1)}), bf16[1,2048,1536]{2,1,0:T(8,128)(2,1)}) %all-gather.5.cloned.1.call-update) | async-done | bytes 6291472 | tf_op jit(solution)/shard_map/all_gather | solution.py:88
  61.1 5.0 %multiply_reduce_fusion.2 = (f32[2048]{0:T(1024)S(1)}, f32[2048,128]{0,1:T(8,128)S(1)}) fusion(bf16[1536,128]{1,0:T(8,128)(2,1)S(1)} %copy-done.11, bf16[1,2048,1536]{2,1,0:T(8,128)(2,1)} %all-gather.5.cloned.1.call-done), kind=kOutput, calls=%fused_computation.81 | convolution fusion | flops 805828608 | bytes 7741440 | tf_op jit(solution)/shard_map/dot_general | solution.py:39
  66.5 4.8 %multiply_reduce_fusion.3 = (f32[2048]{0:T(1024)S(1)}, f32[2048,128]{1,0:T(8,128)S(1)}) fusion(bf16[1536,128]{1,0:T(8,128)(2,1)S(1)} %copy-done, bf16[1,2048,1536]{2,1,0:T(8,128)(2,1)} %all-gather.5.cloned.1.call-done), kind=kOutput, calls=%fused_computation.83 | convolution fusion | flops 805828608 | bytes 7741440 | tf_op jit(solution)/shard_map/dot_general | solution.py:37
  76.9 7.0 %while.37 = (s32[]{:T(128)}, bf16[4,512,1,128]{3,1,2,0:T(8,128)(2,1)S(1)}, bf16[4,512,1,128]{3,1,2,0:T(8,128)(2,1)S(1)}, bf16[2048,1,128]{2,0,1:T(8,128)(2,1)S(1)}, bf16[2048,1,128]{2,0,1:T(8,128)(2,1)S(1)}, /*index=5*/s32[]{:T(128)}) while((s32[]{:T(128)}, bf16[4,512,1,128]{3,1,2,0:T(8,128)(2,1)S(1)}, bf16[4,512,1,128]{3,1,2,0:T(8,128)(2,1)S(1)}, ...), condition=%wide.region_6.0_spmd, body=%wide.region_4.6_spmd.sunk | while | flops 542178816 | bytes 9703501 | solution.py:65
  84.0 8.1 %copy.65 = bf16[1,2048,128]{2,0,1:T(2,128)(2,1)S(1)} copy(bf16[1,2048,128]{2,1,0:T(8,128)(2,1)S(1)} %bitcast.242) | data formatting | bytes 1048576 | tf_op jit(solution)/shard_map/while/body/jit(dynamic_update_index_in_dim)/broadcast_in_dim | solution.py:108
  92.6 11.5 %reduce.21 = bf16[2048,128]{1,0:T(8,128)(2,1)S(1)} reduce(bf16[2048,1,128]{2,1,0:T(2,128)(2,1)S(1)} %bitcast.234, bf16[]{:T(256)} %broadcast.240), dimensions={1}, to_apply=%bitcast.196.reduce_sub_computation | reduce | bytes 1048578
  105.1 5.4 %all-to-all-start = ((bf16[16,2,8192]{2,1,0:T(2,128)(2,1)}), bf16[16,2,8192]{2,1,0:T(2,128)(2,1)}, u32[]{:S(2)}, u32[]{:S(2)}) async-start(bf16[16,2,8192]{2,1,0:T(2,128)(2,1)} %reshape.341), calls=%async_computation | async-start | bytes 1048576 | tf_op jit(solution)/shard_map/all_to_all | solution.py:97
  110.5 31.3 %all-gather.9.cloned.1.call-done = bf16[2,2048,1536]{2,1,0:T(8,128)(2,1)} async-done(((bf16[2,128,1536]{2,1,0:T(8,128)(2,1)}), bf16[2,2048,1536]{2,1,0:T(8,128)(2,1)}) %all-gather.9.cloned.1.call-update) | async-done | bytes 12582928 | tf_op jit(solution)/shard_map/all_gather | solution.py:88
  141.8 6.7 %multiply_reduce_fusion.1 = (f32[4096]{0:T(1024)S(1)}, f32[4096,128]{1,0:T(8,128)S(1)}) fusion(bf16[4096,1536]{1,0:T(8,128)(2,1)} %bitcast.246, bf16[1536,128]{1,0:T(8,128)(2,1)S(1)} %copy-done), kind=kOutput, calls=%fused_computation.63 | convolution fusion | flops 1611657216 | bytes 15089664 | tf_op jit(solution)/shard_map/dot_general | solution.py:37
  150.1 3.5 %multiply_reduce_fusion = (f32[4096]{0:T(1024)S(1)}, f32[4096,128]{1,0:T(8,128)S(1)}) fusion(bf16[4096,1536]{1,0:T(8,128)(2,1)S(1)} %bitcast.247, bf16[1536,128]{1,0:T(8,128)(2,1)S(1)} %copy-done.12), kind=kOutput, calls=%fused_computation.61 | convolution fusion | flops 1611657216 | bytes 15089664 | tf_op jit(solution)/shard_map/dot_general | solution.py:39
  153.7 3.4 convolution_convert_fusion
  160.6 91.0 %all-gather.11.cloned.1.call-done = bf16[8,2048,2,128]{3,1,2,0:T(8,128)(2,1)} async-done(((bf16[1,2048,2,128]{3,1,2,0:T(8,128)(2,1)}), bf16[8,2048,2,128]{3,1,2,0:T(8,128)(2,1)}) %all-gather.11.cloned.1.call-update) | async-done | bytes 8388624 | tf_op jit(solution)/shard_map/all_gather | solution.py:112
  251.6 4.3 %gather_fusion = bf16[2,2048,2,128]{3,1,2,0:T(8,128)(2,1)S(1)} fusion(bf16[8,2048,2,128]{3,1,2,0:T(8,128)(2,1)} %all-gather.11.cloned.1.call-done, s32[1024]{0:T(1024)S(1)} %pad_clamp_fusion), kind=kCustom, calls=%fused_computation | custom fusion | bytes 4194312 | tf_op jit(solution)/shard_map/jit(_take)/gather | solution.py:115
  256.1 2.2 bitcast_select_fusion
  258.2 2.5 reshape.321
  260.7 51.7 %while.39 = (s32[]{:T(128)}, bf16[2,2048,128]{2,1,0:T(8,128)(2,1)}, bf16[2,2048,3,128]{3,1,2,0:T(8,128)(2,1)}, bf16[2,4096,2,128]{3,1,2,0:T(8,128)(2,1)}, s32[]{:T(128)}, /*index=5*/s32[]{:T(128)}, s32[]{:T(128)}) while((s32[]{:T(128)}, bf16[2,2048,128]{2,1,0:T(8,128)(2,1)}, bf16[2,2048,3,128]{3,1,2,0:T(8,128)(2,1)}, ...), condition=%wide.region_15.16_spmd, body=%wide.region_11.15_spmd.sunk | while | flops 1632697856 | bytes 73667344 | solution.py:131
  265.3 20.4 %while.40 = (s32[]{:T(128)}, bf16[4,512,1,128]{3,1,2,0:T(8,128)(2,1)S(1)}, bf16[4,512,1,128]{3,1,2,0:T(8,128)(2,1)S(1)}, bf16[6144,1,128]{2,0,1:T(8,128)(2,1)S(1)}, bf16[6144,1,128]{2,0,1:T(8,128)(2,1)}, /*index=5*/s32[]{:T(128)}) while((s32[]{:T(128)}, bf16[4,512,1,128]{3,1,2,0:T(8,128)(2,1)S(1)}, bf16[4,512,1,128]{3,1,2,0:T(8,128)(2,1)S(1)}, ...), condition=%wide.region_14.14_spmd, body=%wide.region_12.13_spmd.sunk | while | flops 1626406400 | bytes 34869352 | solution.py:65
  267.4 3.1 fusion.115
  272.5 3.1 fusion.115
  277.6 3.1 fusion.115
  282.7 3.1 fusion.115
  291.2 20.4 %while.40 = (s32[]{:T(128)}, bf16[4,512,1,128]{3,1,2,0:T(8,128)(2,1)S(1)}, bf16[4,512,1,128]{3,1,2,0:T(8,128)(2,1)S(1)}, bf16[6144,1,128]{2,0,1:T(8,128)(2,1)S(1)}, bf16[6144,1,128]{2,0,1:T(8,128)(2,1)}, /*index=5*/s32[]{:T(128)}) while((s32[]{:T(128)}, bf16[4,512,1,128]{3,1,2,0:T(8,128)(2,1)S(1)}, bf16[4,512,1,128]{3,1,2,0:T(8,128)(2,1)S(1)}, ...), condition=%wide.region_14.14_spmd, body=%wide.region_12.13_spmd.sunk | while | flops 1626406400 | bytes 34869352 | solution.py:65
  293.2 3.1 fusion.115
  298.3 3.1 fusion.115
  303.4 3.1 fusion.115
  308.6 3.1 fusion.115
  312.5 3.6 %copy.59 = bf16[2,2048,128]{2,0,1:T(2,128)(2,1)} copy(bf16[2,2048,128]{2,1,0:T(8,128)(2,1)} %get-tuple-element.88) | data formatting | bytes 2097152 | tf_op jit(solution)/shard_map/while | solution.py:131
  316.1 5.4 %all-to-all-start.1 = ((bf16[2,2048,128]{2,0,1:T(2,128)(2,1)}), bf16[2,2048,128]{2,0,1:T(2,128)(2,1)S(1)}, u32[]{:S(2)}, u32[]{:S(2)}) async-start(bf16[2,2048,128]{2,0,1:T(2,128)(2,1)} %copy.59), calls=%async_computation.1 | async-start | bytes 2097152 | tf_op jit(solution)/shard_map/all_to_all | solution.py:97
  322.1 2.3 reshape.342
  324.7 4.6 %fusion.52 = bf16[1,128,1536]{2,1,0:T(8,128)(2,1)} fusion(bf16[128,2048]{0,1:T(8,128)(2,1)S(1)} %bitcast.239, bf16[2048,1536]{1,0:T(8,128)(2,1)} %all-gather.7.cloned.1.call-done, bf16[1,128,1536]{2,1,0:T(8,128)(2,1)S(1)} %copy-done.7, f32[1536]{0:T(1024)S(1)} %convolution_reduce_fusion.2), kind=kOutput, calls=%fused_computation.55 | convolution fusion | flops 806092800 | bytes 7608320 | tf_op jit(solution)/shard_map/dot_general | solution.py:99
  329.3 8.1 %all-to-all-done.1 = bf16[2,2048,128]{2,0,1:T(2,128)(2,1)S(1)} async-done(((bf16[2,2048,128]{2,0,1:T(2,128)(2,1)}), bf16[2,2048,128]{2,0,1:T(2,128)(2,1)S(1)}, u32[]{:S(2)}, u32[]{:S(2)}) %all-to-all-start.1) | async-done | bytes 1048608 | tf_op jit(solution)/shard_map/all_to_all | solution.py:97
  338.6 5.5 %fusion.48 = bf16[1,2,128,1536]{3,2,1,0:T(8,128)(2,1)} fusion(bf16[2,128,2048]{2,1,0:T(8,128)(2,1)S(1)} %dot_general.69, bf16[2048,1536]{1,0:T(8,128)(2,1)} %all-gather.7.cloned.1.call-done, bf16[1,2,128,1536]{3,2,1,0:T(8,128)(2,1)S(1)} %copy-done.6, f32[2,1536]{1,0:T(2,128)S(1)} %fusion.77), kind=kOutput, calls=%fused_computation.53 | convolution fusion | flops 1612185600 | bytes 8925184 | tf_op jit(solution)/shard_map/dot_general | solution.py:99
  (147 shorter events, 57.9 us)
Async XLA Ops:
  7.2 59.3 %copy-start = (bf16[1536,128]{1,0:T(8,128)(2,1)S(1)}, bf16[1536,128]{1,0:T(8,128)(2,1)}, u32[]{:S(2)}) copy-start(bf16[1536,128]{1,0:T(8,128)(2,1)} %param.28) | copy-start | bytes 1179652
  7.2 8.0 %copy-start.5 = (bf16[1,2,128,1536]{3,2,1,0:T(8,128)(2,1)S(1)}, bf16[1,2,128,1536]{3,2,1,0:T(8,128)(2,1)}, u32[]{:S(2)}) copy-start(bf16[1,2,128,1536]{3,2,1,0:T(8,128)(2,1)} %param.22) | copy-start | bytes 2359300
  7.2 53.9 %all-gather.5.cloned.1.call-start = ((), (), s32[]{:S(2)}) async-start(), calls=%async_computation.2 | async-start | bytes 6684672 | tf_op jit(solution)/shard_map/all_gather | solution.py:88
  9.2 6.5 %copy-start.8 = (f32[64,1536]{1,0:T(8,128)S(1)}, f32[64,1536]{1,0:T(8,128)}, u32[]{:S(2)}) copy-start(f32[64,1536]{1,0:T(8,128)} %param.26) | copy-start | bytes 1179652
  9.2 6.5 %copy-start.13 = (s32[1,2]{1,0:T(1,128)S(1)}, s32[1,2]{1,0:T(1,128)}, u32[]{:S(2)}) copy-start(s32[1,2]{1,0:T(1,128)} %param.23) | copy-start | bytes 28
  9.3 6.7 %copy-start.9 = (f32[64,1536]{1,0:T(8,128)S(1)}, f32[64,1536]{1,0:T(8,128)}, u32[]{:S(2)}) copy-start(f32[64,1536]{1,0:T(8,128)} %param.25) | copy-start | bytes 1179652
  15.1 126.7 %all-gather.9.cloned.1.call-start = ((), (), s32[]{:S(2)}) async-start(), calls=%async_computation.4 | async-start | bytes 13369344 | tf_op jit(solution)/shard_map/all_gather | solution.py:88
  15.3 45.8 %copy-start.11 = (bf16[1536,128]{1,0:T(8,128)(2,1)S(1)}, bf16[1536,128]{1,0:T(8,128)(2,1)}, u32[]{:S(2)}) copy-start(bf16[1536,128]{1,0:T(8,128)(2,1)} %param.29) | copy-start | bytes 1179652
  17.5 234.1 %all-gather.11.cloned.1.call-start = ((), (), s32[]{:S(2)}) async-start(), calls=%async_computation.5 | async-start | bytes 9437184 | tf_op jit(solution)/shard_map/all_gather | solution.py:112
  66.4 4.9 %copy-start.4 = (bf16[1,2048,1536]{2,1,0:T(8,128)(2,1)S(1)}, bf16[1,2048,1536]{2,1,0:T(8,128)(2,1)}, u32[]{:S(2)}) copy-start(bf16[1,2048,1536]{2,1,0:T(8,128)(2,1)} %all-gather.5.cloned.1.call-done) | copy-start | bytes 18874372
  66.5 4.9 %copy-start.20 = (bf16[1536,128]{1,0:T(8,128)(2,1)S(1)}, bf16[1536,128]{1,0:T(8,128)(2,1)}, u32[]{:S(2)}) copy-start(bf16[1536,128]{1,0:T(8,128)(2,1)} %param.30) | copy-start | bytes 1179652
  71.3 2.2 copy-start.17
  75.2 249.6 %all-gather.7.cloned.1.call-start = ((), (), s32[]{:S(2)}) async-start(), calls=%async_computation.3 | async-start | bytes 6684672 | tf_op jit(solution)/shard_map/all_gather | solution.py:84
  105.1 211.0 %all-to-all-start = ((bf16[16,2,8192]{2,1,0:T(2,128)(2,1)}), bf16[16,2,8192]{2,1,0:T(2,128)(2,1)}, u32[]{:S(2)}, u32[]{:S(2)}) async-start(bf16[16,2,8192]{2,1,0:T(2,128)(2,1)} %reshape.341), calls=%async_computation | async-start | bytes 1048576 | tf_op jit(solution)/shard_map/all_to_all | solution.py:97
  141.8 6.7 %copy-start.12 = (bf16[1536,128]{1,0:T(8,128)(2,1)S(1)}, bf16[1536,128]{1,0:T(8,128)(2,1)}, u32[]{:S(2)}) copy-start(bf16[1536,128]{1,0:T(8,128)(2,1)} %param.29) | copy-start | bytes 1179652
  141.8 8.3 %copy-start.19 = (bf16[2,2048,1536]{2,1,0:T(8,128)(2,1)S(1)}, bf16[2,2048,1536]{2,1,0:T(8,128)(2,1)}, u32[]{:S(2)}) copy-start(bf16[2,2048,1536]{2,1,0:T(8,128)(2,1)} %all-gather.9.cloned.1.call-done) | copy-start | bytes 37748740
  150.1 3.5 %copy-start.21 = (bf16[1536,128]{1,0:T(8,128)(2,1)S(1)}, bf16[1536,128]{1,0:T(8,128)(2,1)}, u32[]{:S(2)}) copy-start(bf16[1536,128]{1,0:T(8,128)(2,1)} %param.30) | copy-start | bytes 1179652
  153.6 3.5 copy-start.16
  260.9 2.7 copy-start.2
  270.4 2.0 copy-start.3
  275.6 2.0 copy-start.3
  280.7 2.0 copy-start.3
  286.6 2.8 copy-start.2
  291.2 2.0 copy-start.3
  296.3 2.0 copy-start.3
  301.4 2.0 copy-start.3
  306.5 2.0 copy-start.3
  312.5 9.1 %copy-start.10 = (f32[64,1536]{1,0:T(8,128)S(1)}, f32[64,1536]{1,0:T(8,128)}, u32[]{:S(2)}) copy-start(f32[64,1536]{1,0:T(8,128)} %param.27) | copy-start | bytes 1179652
  312.5 9.3 %copy-start.14 = (s32[1,2]{1,0:T(1,128)S(1)}, s32[1,2]{1,0:T(1,128)}, u32[]{:S(2)}) copy-start(s32[1,2]{1,0:T(1,128)} %param.23) | copy-start | bytes 28
  316.1 21.2 %all-to-all-start.1 = ((bf16[2,2048,128]{2,0,1:T(2,128)(2,1)}), bf16[2,2048,128]{2,0,1:T(2,128)(2,1)S(1)}, u32[]{:S(2)}, u32[]{:S(2)}) async-start(bf16[2,2048,128]{2,0,1:T(2,128)(2,1)} %copy.59), calls=%async_computation.1 | async-start | bytes 2097152 | tf_op jit(solution)/shard_map/all_to_all | solution.py:97
  322.1 2.7 copy-start.7
  338.5 5.5 %copy-start.1 = (bf16[1536,128]{1,0:T(8,128)(2,1)S(1)}, bf16[1536,128]{1,0:T(8,128)(2,1)}, u32[]{:S(2)}) copy-start(bf16[1536,128]{1,0:T(8,128)(2,1)} %param.28) | copy-start | bytes 1179652
  (5 other events, 7.5 us)
Sparse Core Ops, SparseCore 0:
  15.2 45.8 all-gather.4
  63.3 78.4 all-gather.8
  144.2 107.3 all-gather.10
  253.1 40.8 all-gather.6
where the time goes:
time: 357 us; the launch traced here: 351 us
  waiting for transfers between devices  174 us (49%)
  matrix products  86.5 us (24%)
  local copies, waits for them, and re-layouts  34.9 us (10%)
  other arithmetic  28.3 us (8%)
  between operations  15.3 us (4%)
  starting transfers between devices  11.5 us (3%)
    all_gather x1, waiting for transfers between devices, local(): cond_all = lax.all_gather(key_heads[:, :, 1:], 'seg', axis=0, tiled=True)  91 us
    all_gather x2, waiting for transfers between devices, to_heads(): lax.all_gather(modded, 'seq', axis=1, tiled=True)  74.8 us
    dot_general x12, matrix products, one_block(): jnp.einsum('hqk,khd->qhd', weights, value_heads, preferred_element_type=j...  28 us
    dot_general x12, matrix products, one_block(): jnp.einsum('qhd,khd->hqk', queries, key_heads, preferred_element_type=jnp...  19.6 us
    unnamed x1, other arithmetic  11.5 us
    dot_general x2, matrix products, project(): jnp.dot(flat, query_weight, preferred_element_type=jnp.float32)  11.5 us
    all_to_all x2, starting transfers between devices, finish(): lax.all_to_all(heads_out, 'seq', split_axis=1, concat_axis=2, tiled=True)  10.8 us
    dot_general x2, matrix products, finish(): jnp.dot(token_side.reshape(frames * tokens, columns), out_full, preferred...  10.1 us
  transfers between devices with their start and end apart: 6, of which 4 were waited for; matrix products, arithmetic and copies ran while one was open for 38% of the time, Pallas kernels for 0%

commit v1 on v0

--- a/solution.py
+++ b/solution.py
@@ -109,7 +109,9 @@
         lambda frame_data: attend(frame_data[:, 0], frame_data[:, 1], frame_data[:, 2]), key_heads
     )
     keyframe_out = finish(keyframe_latents, keyframe_steps, key_att)
-    cond_all = lax.all_gather(key_heads[:, :, 1:], "seg", axis=0, tiled=True)
+    cond_all = jnp.concatenate(
+        lax.all_to_all(jnp.stack([key_heads[:, :, 1:]] * lax.axis_size("seg")), "seg", 0, 0), axis=0
+    )
     segment_count = bounds.shape[0]
     length = cond_all.shape[1]
     picked = jnp.take(cond_all, bounds.reshape(-1), axis=0)

time: 357 us -> 384 us (1.076)
  waiting for transfers between devices: 174 us -> 189 us
  starting transfers between devices: 11.5 us -> 18.7 us
    all_to_all x0 -> x1, waiting for transfers between devices: none -> 137 us  [local(): lax.all_to_all(jnp.stack([key_heads[:, :, 1:]] * lax.axis_size('seg')), '...]
    all_gather x1 -> x0, waiting for transfers between devices: 91 us -> none  [local(): cond_all = lax.all_gather(key_heads[:, :, 1:], 'seg', axis=0, tiled=True)]
    all_gather x2, waiting for transfers between devices: 74.8 us -> 43.6 us  [to_heads(): lax.all_gather(modded, 'seq', axis=1, tiled=True)]
    all_to_all x0 -> x1, starting transfers between devices: none -> 6.69 us  [local(): lax.all_to_all(jnp.stack([key_heads[:, :, 1:]] * lax.axis_size('seg')), '...]
    another operation x0 -> x1, local copies, waits for them, and re-layouts: none -> 4.87 us  [local(): jnp.stack([key_heads[:, :, 1:]] * lax.axis_size('seg'))]
  transfers between devices with their start and end apart: 6 -> 6, of which waited for: 4 -> 3; matrix products, arithmetic and copies ran while one was open for 38% -> 36% of each run, Pallas kernels for 0% -> 0%
where the time goes in v1:
time: 384 us; the launch traced here: 377 us
  waiting for transfers between devices  189 us (49%)
  matrix products  86.5 us (23%)
  local copies, waits for them, and re-layouts  38.6 us (10%)
  other arithmetic  28.2 us (7%)
  starting transfers between devices  18.7 us (5%)
  between operations  15.3 us (4%)
    all_to_all x1, waiting for transfers between devices, local(): lax.all_to_all(jnp.stack([key_heads[:, :, 1:]] * lax.axis_size('seg')), '...  137 us
    all_gather x2, waiting for transfers between devices, to_heads(): lax.all_gather(modded, 'seq', axis=1, tiled=True)  43.6 us
    dot_general x12, matrix products, one_block(): jnp.einsum('hqk,khd->qhd', weights, value_heads, preferred_element_type=j...  28.1 us
    dot_general x12, matrix products, one_block(): jnp.einsum('qhd,khd->hqk', queries, key_heads, preferred_element_type=jnp...  19.6 us
    unnamed x1, other arithmetic  11.5 us
    dot_general x2, matrix products, project(): jnp.dot(flat, query_weight, preferred_element_type=jnp.float32)  11.5 us
    all_to_all x2, starting transfers between devices, finish(): lax.all_to_all(heads_out, 'seq', split_axis=1, concat_axis=2, tiled=True)  11.5 us
    dot_general x2, matrix products, finish(): jnp.dot(token_side.reshape(frames * tokens, columns), out_full, preferred...  10.1 us
  transfers between devices with their start and end apart: 6, of which 3 were waited for; matrix products, arithmetic and copies ran while one was open for 36% of the time, Pallas kernels for 0%

profile of v1, /device:TPU:1, one launch (start us, length us, event | category | flops | bytes accessed | tf_op | source)
XLA Modules:
  0.0 377.2 jit_solution(7273438107911995754)
XLA Ops:
  17.5 43.6 %all-gather.4.cloned.1.call-done = bf16[1,2048,1536]{2,1,0:T(8,128)(2,1)} async-done(((bf16[1,128,1536]{2,1,0:T(8,128)(2,1)}), bf16[1,2048,1536]{2,1,0:T(8,128)(2,1)}) %all-gather.4.cloned.1.call-update) | async-done | bytes 6291472 | tf_op jit(solution)/shard_map/all_gather | solution.py:88
  61.1 5.0 %multiply_reduce_fusion.2 = (f32[2048]{0:T(1024)S(1)}, f32[2048,128]{0,1:T(8,128)S(1)}) fusion(bf16[1536,128]{1,0:T(8,128)(2,1)S(1)} %copy-done.11, bf16[1,2048,1536]{2,1,0:T(8,128)(2,1)} %all-gather.4.cloned.1.call-done), kind=kOutput, calls=%fused_computation.82 | convolution fusion | flops 805828608 | bytes 7741440 | tf_op jit(solution)/shard_map/dot_general | solution.py:39
  66.5 4.8 %multiply_reduce_fusion.3 = (f32[2048]{0:T(1024)S(1)}, f32[2048,128]{1,0:T(8,128)S(1)}) fusion(bf16[1536,128]{1,0:T(8,128)(2,1)S(1)} %copy-done, bf16[1,2048,1536]{2,1,0:T(8,128)(2,1)} %all-gather.4.cloned.1.call-done), kind=kOutput, calls=%fused_computation.84 | convolution fusion | flops 805828608 | bytes 7741440 | tf_op jit(solution)/shard_map/dot_general | solution.py:37
  74.1 4.9 %stack.14 = bf16[8,1,2048,2,128]{4,2,3,1,0:T(8,128)(2,1)} broadcast(bf16[2048,2,128]{2,0,1:T(8,128)(2,1)S(1)} %slice_bitcast_fusion.4), dimensions={2,3,4} | broadcast | bytes 9437184 | tf_op jit(solution)/shard_map/stack | solution.py:113
  79.0 6.7 %all-to-all-start.1 = ((bf16[8,1,2048,2,128]{4,2,3,1,0:T(8,128)(2,1)}), bf16[8,1,2048,2,128]{4,2,3,1,0:T(8,128)(2,1)}, u32[]{:S(2)}, u32[]{:S(2)}) async-start(bf16[8,1,2048,2,128]{4,2,3,1,0:T(8,128)(2,1)} %stack.14), calls=%async_computation.1 | async-start | bytes 16777216 | tf_op jit(solution)/shard_map/all_to_all | solution.py:113
  87.6 7.0 %while.37 = (s32[]{:T(128)}, bf16[4,512,1,128]{3,1,2,0:T(8,128)(2,1)S(1)}, bf16[4,512,1,128]{3,1,2,0:T(8,128)(2,1)S(1)}, bf16[2048,1,128]{2,0,1:T(8,128)(2,1)S(1)}, bf16[2048,1,128]{2,0,1:T(8,128)(2,1)S(1)}, /*index=5*/s32[]{:T(128)}) while((s32[]{:T(128)}, bf16[4,512,1,128]{3,1,2,0:T(8,128)(2,1)S(1)}, bf16[4,512,1,128]{3,1,2,0:T(8,128)(2,1)S(1)}, ...), condition=%wide.region_6.0_spmd, body=%wide.region_4.6_spmd.sunk | while | flops 542178816 | bytes 9703501 | solution.py:65
  94.6 8.1 %copy.66 = bf16[1,2048,128]{2,0,1:T(2,128)(2,1)S(1)} copy(bf16[1,2048,128]{2,1,0:T(8,128)(2,1)S(1)} %bitcast.245) | data formatting | bytes 1048576 | tf_op jit(solution)/shard_map/while/body/jit(dynamic_update_index_in_dim)/broadcast_in_dim | solution.py:108
  103.3 11.5 %reduce.21 = bf16[2048,128]{1,0:T(8,128)(2,1)S(1)} reduce(bf16[2048,1,128]{2,1,0:T(2,128)(2,1)S(1)} %bitcast.237, bf16[]{:T(256)} %broadcast.243), dimensions={1}, to_apply=%bitcast.199.reduce_sub_computation | reduce | bytes 1048578
  115.8 137.4 %all-to-all-done.1 = bf16[8,1,2048,2,128]{4,2,3,1,0:T(8,128)(2,1)} async-done(((bf16[8,1,2048,2,128]{4,2,3,1,0:T(8,128)(2,1)}), bf16[8,1,2048,2,128]{4,2,3,1,0:T(8,128)(2,1)}, u32[]{:S(2)}, u32[]{:S(2)}) %all-to-all-start.1) | async-done | bytes 8388640 | tf_op jit(solution)/shard_map/all_to_all | solution.py:113
  253.1 5.7 %all-to-all-start = ((bf16[16,2,8192]{2,1,0:T(2,128)(2,1)}), bf16[16,2,8192]{2,1,0:T(2,128)(2,1)}, u32[]{:S(2)}, u32[]{:S(2)}) async-start(bf16[16,2,8192]{2,1,0:T(2,128)(2,1)} %reshape.348), calls=%async_computation | async-start | bytes 1048576 | tf_op jit(solution)/shard_map/all_to_all | solution.py:97
  258.9 4.3 %gather_fusion = bf16[2,2048,2,128]{3,1,2,0:T(8,128)(2,1)S(1)} fusion(bf16[8,2048,2,128]{3,1,2,0:T(8,128)(2,1)} %bitcast.51, s32[1024]{0:T(1024)S(1)} %pad_clamp_fusion), kind=kCustom, calls=%fused_computation | custom fusion | bytes 4194312 | tf_op jit(solution)/shard_map/jit(_take)/gather | solution.py:117
  265.6 6.7 %multiply_reduce_fusion.1 = (f32[4096]{0:T(1024)S(1)}, f32[4096,128]{1,0:T(8,128)S(1)}) fusion(bf16[4096,1536]{1,0:T(8,128)(2,1)} %bitcast.249, bf16[1536,128]{1,0:T(8,128)(2,1)S(1)} %copy-done), kind=kOutput, calls=%fused_computation.63 | convolution fusion | flops 1611657216 | bytes 15089664 | tf_op jit(solution)/shard_map/dot_general | solution.py:37
  273.9 3.5 multiply_reduce_fusion
  277.4 3.4 convolution_convert_fusion
  284.4 2.5 reshape.328
  286.9 51.6 %while.39 = (s32[]{:T(128)}, bf16[2,2048,128]{2,1,0:T(8,128)(2,1)}, bf16[2,2048,3,128]{3,1,2,0:T(8,128)(2,1)}, bf16[2,4096,2,128]{3,1,2,0:T(8,128)(2,1)}, s32[]{:T(128)}, /*index=5*/s32[]{:T(128)}, s32[]{:T(128)}) while((s32[]{:T(128)}, bf16[2,2048,128]{2,1,0:T(8,128)(2,1)}, bf16[2,2048,3,128]{3,1,2,0:T(8,128)(2,1)}, ...), condition=%wide.region_15.16_spmd, body=%wide.region_11.15_spmd.sunk | while | flops 1632697856 | bytes 73667344 | solution.py:133
  291.5 20.4 %while.40 = (s32[]{:T(128)}, bf16[4,512,1,128]{3,1,2,0:T(8,128)(2,1)S(1)}, bf16[4,512,1,128]{3,1,2,0:T(8,128)(2,1)S(1)}, bf16[6144,1,128]{2,0,1:T(8,128)(2,1)S(1)}, bf16[6144,1,128]{2,0,1:T(8,128)(2,1)}, /*index=5*/s32[]{:T(128)}) while((s32[]{:T(128)}, bf16[4,512,1,128]{3,1,2,0:T(8,128)(2,1)S(1)}, bf16[4,512,1,128]{3,1,2,0:T(8,128)(2,1)S(1)}, ...), condition=%wide.region_14.14_spmd, body=%wide.region_12.13_spmd.sunk | while | flops 1626406400 | bytes 34869352 | solution.py:65
  293.5 3.1 fusion.115
  298.6 3.1 fusion.115
  303.7 3.1 fusion.115
  308.9 3.1 fusion.115
  317.2 20.5 %while.40 = (s32[]{:T(128)}, bf16[4,512,1,128]{3,1,2,0:T(8,128)(2,1)S(1)}, bf16[4,512,1,128]{3,1,2,0:T(8,128)(2,1)S(1)}, bf16[6144,1,128]{2,0,1:T(8,128)(2,1)S(1)}, bf16[6144,1,128]{2,0,1:T(8,128)(2,1)}, /*index=5*/s32[]{:T(128)}) while((s32[]{:T(128)}, bf16[4,512,1,128]{3,1,2,0:T(8,128)(2,1)S(1)}, bf16[4,512,1,128]{3,1,2,0:T(8,128)(2,1)S(1)}, ...), condition=%wide.region_14.14_spmd, body=%wide.region_12.13_spmd.sunk | while | flops 1626406400 | bytes 34869352 | solution.py:65
  319.2 3.1 fusion.115
  324.3 3.1 fusion.115
  329.4 3.1 fusion.115
  334.6 3.1 fusion.115
  338.5 3.7 copy.60
  342.1 5.7 %all-to-all-start.2 = ((bf16[2,2048,128]{2,0,1:T(2,128)(2,1)}), bf16[2,2048,128]{2,0,1:T(2,128)(2,1)S(1)}, u32[]{:S(2)}, u32[]{:S(2)}) async-start(bf16[2,2048,128]{2,0,1:T(2,128)(2,1)} %copy.60), calls=%async_computation.2 | async-start | bytes 2097152 | tf_op jit(solution)/shard_map/all_to_all | solution.py:97
  348.4 2.3 reshape.349
  351.1 4.6 %fusion.52 = bf16[1,128,1536]{2,1,0:T(8,128)(2,1)} fusion(bf16[128,2048]{0,1:T(8,128)(2,1)S(1)} %bitcast.242, bf16[2048,1536]{1,0:T(8,128)(2,1)} %all-gather.6.cloned.1.call-done, bf16[1,128,1536]{2,1,0:T(8,128)(2,1)S(1)} %copy-done.7, f32[1536]{0:T(1024)S(1)} %convolution_reduce_fusion.2), kind=kOutput, calls=%fused_computation.55 | convolution fusion | flops 806092800 | bytes 7608320 | tf_op jit(solution)/shard_map/dot_general | solution.py:99
  355.6 8.1 %all-to-all-done.2 = bf16[2,2048,128]{2,0,1:T(2,128)(2,1)S(1)} async-done(((bf16[2,2048,128]{2,0,1:T(2,128)(2,1)}), bf16[2,2048,128]{2,0,1:T(2,128)(2,1)S(1)}, u32[]{:S(2)}, u32[]{:S(2)}) %all-to-all-start.2) | async-done | bytes 1048608 | tf_op jit(solution)/shard_map/all_to_all | solution.py:97
  364.9 5.5 %fusion.48 = bf16[1,2,128,1536]{3,2,1,0:T(8,128)(2,1)} fusion(bf16[2,128,2048]{2,1,0:T(8,128)(2,1)S(1)} %dot_general.69, bf16[2048,1536]{1,0:T(8,128)(2,1)} %all-gather.6.cloned.1.call-done, bf16[1,2,128,1536]{3,2,1,0:T(8,128)(2,1)S(1)} %copy-done.6, f32[2,1536]{1,0:T(2,128)S(1)} %fusion.77), kind=kOutput, calls=%fused_computation.53 | convolution fusion | flops 1612185600 | bytes 8925184 | tf_op jit(solution)/shard_map/dot_general | solution.py:99
  (147 shorter events, 58.9 us)
Async XLA Ops:
  7.2 59.3 %copy-start = (bf16[1536,128]{1,0:T(8,128)(2,1)S(1)}, bf16[1536,128]{1,0:T(8,128)(2,1)}, u32[]{:S(2)}) copy-start(bf16[1536,128]{1,0:T(8,128)(2,1)} %param.28) | copy-start | bytes 1179652
  7.2 8.0 %copy-start.5 = (bf16[1,2,128,1536]{3,2,1,0:T(8,128)(2,1)S(1)}, bf16[1,2,128,1536]{3,2,1,0:T(8,128)(2,1)}, u32[]{:S(2)}) copy-start(bf16[1,2,128,1536]{3,2,1,0:T(8,128)(2,1)} %param.22) | copy-start | bytes 2359300
  7.2 53.9 %all-gather.4.cloned.1.call-start = ((), (), s32[]{:S(2)}) async-start(), calls=%async_computation.3 | async-start | bytes 6684672 | tf_op jit(solution)/shard_map/all_gather | solution.py:88
  9.2 6.5 %copy-start.8 = (f32[64,1536]{1,0:T(8,128)S(1)}, f32[64,1536]{1,0:T(8,128)}, u32[]{:S(2)}) copy-start(f32[64,1536]{1,0:T(8,128)} %param.26) | copy-start | bytes 1179652
  9.2 6.5 %copy-start.13 = (s32[1,2]{1,0:T(1,128)S(1)}, s32[1,2]{1,0:T(1,128)}, u32[]{:S(2)}) copy-start(s32[1,2]{1,0:T(1,128)} %param.23) | copy-start | bytes 28
  9.3 6.7 %copy-start.9 = (f32[64,1536]{1,0:T(8,128)S(1)}, f32[64,1536]{1,0:T(8,128)}, u32[]{:S(2)}) copy-start(f32[64,1536]{1,0:T(8,128)} %param.25) | copy-start | bytes 1179652
  15.1 250.5 %all-gather.8.cloned.1.call-start = ((), (), s32[]{:S(2)}) async-start(), calls=%async_computation.5 | async-start | bytes 13369344 | tf_op jit(solution)/shard_map/all_gather | solution.py:88
  15.3 45.8 %copy-start.11 = (bf16[1536,128]{1,0:T(8,128)(2,1)S(1)}, bf16[1536,128]{1,0:T(8,128)(2,1)}, u32[]{:S(2)}) copy-start(bf16[1536,128]{1,0:T(8,128)(2,1)} %param.29) | copy-start | bytes 1179652
  66.4 4.9 %copy-start.4 = (bf16[1,2048,1536]{2,1,0:T(8,128)(2,1)S(1)}, bf16[1,2048,1536]{2,1,0:T(8,128)(2,1)}, u32[]{:S(2)}) copy-start(bf16[1,2048,1536]{2,1,0:T(8,128)(2,1)} %all-gather.4.cloned.1.call-done) | copy-start | bytes 18874372
  66.5 4.9 %copy-start.20 = (bf16[1536,128]{1,0:T(8,128)(2,1)S(1)}, bf16[1536,128]{1,0:T(8,128)(2,1)}, u32[]{:S(2)}) copy-start(bf16[1536,128]{1,0:T(8,128)(2,1)} %param.30) | copy-start | bytes 1179652
  71.3 2.2 copy-start.17
  79.0 7.4 %copy-start.22 = (s32[1,2]{1,0:T(1,128)S(1)}, s32[1,2]{1,0:T(1,128)}, u32[]{:S(2)}) copy-start(s32[1,2]{1,0:T(1,128)} %param.24) | copy-start | bytes 28
  79.0 174.1 %all-to-all-start.1 = ((bf16[8,1,2048,2,128]{4,2,3,1,0:T(8,128)(2,1)}), bf16[8,1,2048,2,128]{4,2,3,1,0:T(8,128)(2,1)}, u32[]{:S(2)}, u32[]{:S(2)}) async-start(bf16[8,1,2048,2,128]{4,2,3,1,0:T(8,128)(2,1)} %stack.14), calls=%async_computation.1 | async-start | bytes 16777216 | tf_op jit(solution)/shard_map/all_to_all | solution.py:113
  85.7 265.4 %all-gather.6.cloned.1.call-start = ((), (), s32[]{:S(2)}) async-start(), calls=%async_computation.4 | async-start | bytes 6684672 | tf_op jit(solution)/shard_map/all_gather | solution.py:84
  253.1 89.0 %all-to-all-start = ((bf16[16,2,8192]{2,1,0:T(2,128)(2,1)}), bf16[16,2,8192]{2,1,0:T(2,128)(2,1)}, u32[]{:S(2)}, u32[]{:S(2)}) async-start(bf16[16,2,8192]{2,1,0:T(2,128)(2,1)} %reshape.348), calls=%async_computation | async-start | bytes 1048576 | tf_op jit(solution)/shard_map/all_to_all | solution.py:97
  265.6 6.7 %copy-start.12 = (bf16[1536,128]{1,0:T(8,128)(2,1)S(1)}, bf16[1536,128]{1,0:T(8,128)(2,1)}, u32[]{:S(2)}) copy-start(bf16[1536,128]{1,0:T(8,128)(2,1)} %param.29) | copy-start | bytes 1179652
  265.6 8.3 %copy-start.19 = (bf16[2,2048,1536]{2,1,0:T(8,128)(2,1)S(1)}, bf16[2,2048,1536]{2,1,0:T(8,128)(2,1)}, u32[]{:S(2)}) copy-start(bf16[2,2048,1536]{2,1,0:T(8,128)(2,1)} %all-gather.8.cloned.1.call-done) | copy-start | bytes 37748740
  273.9 3.5 copy-start.21
  277.4 3.5 copy-start.16
  287.1 2.7 copy-start.2
  296.6 2.0 copy-start.3
  301.7 2.0 copy-start.3
  306.8 2.0 copy-start.3
  312.8 2.7 copy-start.2
  322.3 2.0 copy-start.3
  327.4 2.0 copy-start.3
  332.5 2.0 copy-start.3
  338.5 9.4 %copy-start.10 = (f32[64,1536]{1,0:T(8,128)S(1)}, f32[64,1536]{1,0:T(8,128)}, u32[]{:S(2)}) copy-start(f32[64,1536]{1,0:T(8,128)} %param.27) | copy-start | bytes 1179652
  338.5 9.7 %copy-start.14 = (s32[1,2]{1,0:T(1,128)S(1)}, s32[1,2]{1,0:T(1,128)}, u32[]{:S(2)}) copy-start(s32[1,2]{1,0:T(1,128)} %param.23) | copy-start | bytes 28
  342.1 21.6 %all-to-all-start.2 = ((bf16[2,2048,128]{2,0,1:T(2,128)(2,1)}), bf16[2,2048,128]{2,0,1:T(2,128)(2,1)S(1)}, u32[]{:S(2)}, u32[]{:S(2)}) async-start(bf16[2,2048,128]{2,0,1:T(2,128)(2,1)} %copy.60), calls=%async_computation.2 | async-start | bytes 2097152 | tf_op jit(solution)/shard_map/all_to_all | solution.py:97
  348.4 2.7 copy-start.7
  364.9 5.5 %copy-start.1 = (bf16[1536,128]{1,0:T(8,128)(2,1)S(1)}, bf16[1536,128]{1,0:T(8,128)(2,1)}, u32[]{:S(2)}) copy-start(bf16[1536,128]{1,0:T(8,128)(2,1)} %param.28) | copy-start | bytes 1179652
  (5 other events, 7.9 us)
Sparse Core Ops, SparseCore 0:
  15.2 45.8 all-gather.3
  63.3 119.5 all-gather.7
  184.6 70.6 all-gather.5
